TPU v7x, 32 devices: a whole 2x2x4 slice. The times are simulated.
32 devices in a mesh: grp: 4 (over y, x), seq: 8 (over z, core).
Axes of the slice: x: 2, y: 2, z: 4, core: 2. Of those that a mesh axis runs over, the one named last changes fastest.
Arguments:
- queries: bfloat16 [4096, 3072], P(('grp', 'seq')), may hold values from -130 to 130
- keys: bfloat16 [4096, 192], P(('grp', 'seq')), may hold values from -6 to 6
- values: bfloat16 [4096, 128], P(('grp', 'seq')), may hold values from -6 to 6
- comp_key_weight: float32 [16, 192], replicated, may hold values from -1.5 to 1.5
- comp_value_weight: float32 [16, 128], replicated, may hold values from -1.5 to 1.5
- select: int32 [64, 16], P(('grp', 'seq')), may hold values from 0 to 63, as said below
- gate_logits: float32 [4096, 48], P(('grp', 'seq')), may hold values from -6 to 6
Outputs:
- attended: bfloat16 [4096, 2048], P(('grp', 'seq'))
Inputs may be any that keep to these rules, and one draw needn't show every extreme that they name: select[i, 0] = i; every entry is at most i. Devices are numbered grp index times 8 plus seq index, and a device holds 2 consecutive blocks. Every entry lies on a block held by the tile's own device, by a device of the same group, or by a device of the previous group. Of the tiles of one device, all entries that fall off that device and on devices of one seq index name the same block.
All inputs are finite; a program needn't handle non-finite values.
Results may differ from a plain program's by a relative error of at most 0.0046.
Values may be sent and summed in bfloat16 or wider, within the bound.
A program may use at most 128 MiB of HBM per device.

v0:
```python
import functools

import jax
import jax.numpy as jnp
from jax import lax
from jax.experimental import pallas as pl
from jax.experimental.pallas import tpu as pltpu
from jax.sharding import PartitionSpec as P

WINDOW = 512
LANES = 128
MESH = pl.DeviceIdType.MESH


def padded(width):
    return -(-width // LANES) * LANES


def exchange_kernel(
    groups, within, keys, values, key_weight, value_weight, table, comp,
    packed, comp_own, recv_rows, recv_comp, along_rows, along_comp,
    pair_rows, pair_comp, next_rows, next_comp, local_sem,
):
    group = lax.axis_index("grp")
    seq = lax.axis_index("seq")
    half = within // 2
    sibling = seq + 1 - 2 * lax.rem(seq, 2)
    key_dim = keys.shape[1]
    value_dim = values.shape[1]
    key_room = padded(key_dim)
    stride = key_weight.shape[0]
    comp_rows = keys.shape[0] // stride

    def same_parity(distance):
        return lax.rem(seq + 2 * distance + 2 * within, within)

    barrier = pltpu.get_barrier_semaphore()

    def greet(distance, carry):
        pl.semaphore_signal(
            barrier, inc=1, device_id=(group, same_parity(distance)), device_id_type=MESH
        )
        return carry

    lax.fori_loop(1, half, greet, 0)
    pl.semaphore_signal(barrier, inc=1, device_id=(group, sibling), device_id_type=MESH)
    for step in range(1, groups):
        other = lax.rem(group + step, groups)
        pl.semaphore_signal(barrier, inc=1, device_id=(other, seq), device_id_type=MESH)

    packed[:, :key_room] = jnp.zeros((keys.shape[0], key_room), packed.dtype)
    packed[:, :key_dim] = keys[...]
    packed[:, key_room:] = values[...]
    comp_own[...] = jnp.zeros_like(comp_own)

    def summed(source, weight):
        wide = source[...].astype(jnp.float32).reshape(comp_rows, stride, source.shape[1])
        return jnp.sum(wide * weight[...][None], axis=1)

    comp_own[:, :key_dim] = summed(keys, key_weight)
    comp_own[:, key_room:] = summed(values, value_weight)
    pl.semaphore_wait(barrier, half - 1 + 1 + groups - 1)

    def rows_copy(source, slot, send_sem, target):
        return pltpu.make_async_remote_copy(
            src_ref=source, dst_ref=table.at[slot], send_sem=send_sem,
            recv_sem=recv_rows.at[slot], device_id=target, device_id_type=MESH,
        )

    def comp_copy(source, slot, send_sem, target):
        return pltpu.make_async_remote_copy(
            src_ref=source, dst_ref=comp.at[slot], send_sem=send_sem,
            recv_sem=recv_comp.at[slot], device_id=target, device_id_type=MESH,
        )

    own_slot = within + seq
    own_comp = group * within + seq

    def to_next_groups(rows_source, comp_source, member):
        @pl.when(group < groups - 1)
        def _():
            rows_copy(rows_source, member, next_rows.at[member], (group + 1, seq)).start()

        for step in range(1, groups):
            @pl.when(group + step < groups)
            def _():
                comp_copy(
                    comp_source, group * within + member,
                    next_comp.at[step * within + member], (group + step, seq),
                ).start()

    def spread(distance, carry):
        target = (group, same_parity(distance))
        rows_copy(packed, own_slot, along_rows.at[distance], target).start()
        comp_copy(comp_own, own_comp, along_comp.at[distance], target).start()
        return carry

    lax.fori_loop(1, half, spread, 0)
    to_next_groups(packed, comp_own, seq)
    rows_copy(packed, own_slot, pair_rows.at[own_slot], (group, sibling)).start()
    comp_copy(comp_own, own_comp, pair_comp.at[own_comp], (group, sibling)).start()
    keep_rows = pltpu.make_async_copy(packed, table.at[own_slot], local_sem.at[0])
    keep_comp = pltpu.make_async_copy(comp_own, comp.at[own_comp], local_sem.at[1])
    keep_rows.start()
    keep_comp.start()

    def arrive_rows(slot):
        rows_copy(packed, slot, pair_rows.at[slot], (group, sibling)).wait_recv()

    def arrive_comp(slot):
        comp_copy(comp_own, slot, pair_comp.at[slot], (group, sibling)).wait_recv()

    def pass_rows(slot):
        arrive_rows(slot)
        rows_copy(table.at[slot], slot, pair_rows.at[slot], (group, sibling)).start()

    def pass_comp(slot):
        arrive_comp(slot)
        comp_copy(comp.at[slot], slot, pair_comp.at[slot], (group, sibling)).start()

    def relay(distance, carry):
        member = same_parity(-distance)
        slot = within + member
        comp_slot = group * within + member
        arrive_rows(slot)
        arrive_comp(comp_slot)
        to_next_groups(table.at[slot], comp.at[comp_slot], member)
        rows_copy(table.at[slot], slot, pair_rows.at[slot], (group, sibling)).start()
        comp_copy(comp.at[comp_slot], comp_slot, pair_comp.at[comp_slot], (group, sibling)).start()
        return carry

    lax.fori_loop(1, half, relay, 0)

    def relay_prior(distance, carry):
        member = same_parity(-distance)

        @pl.when(group > 0)
        def _():
            pass_rows(member)

        for step in range(1, groups):
            @pl.when(group >= step)
            def _():
                pass_comp((group - step) * within + member)

        return carry

    lax.fori_loop(0, half, relay_prior, 0)

    def finish(distance, carry):
        member = same_parity(distance)
        other = member + sibling - seq
        arrive_rows(within + other)
        arrive_comp(group * within + other)
        rows_copy(packed, within + member, pair_rows.at[within + member], (group, sibling)).wait_send()
        comp_copy(
            comp_own, group * within + member, pair_comp.at[group * within + member], (group, sibling)
        ).wait_send()

        @pl.when(group > 0)
        def _():
            arrive_rows(other)
            rows_copy(packed, member, pair_rows.at[member], (group, sibling)).wait_send()

        for step in range(1, groups):
            @pl.when(group >= step)
            def _():
                arrive_comp((group - step) * within + other)
                slot = (group - step) * within + member
                comp_copy(comp_own, slot, pair_comp.at[slot], (group, sibling)).wait_send()

        @pl.when(group < groups - 1)
        def _():
            rows_copy(packed, member, next_rows.at[member], (group + 1, seq)).wait_send()

        for step in range(1, groups):
            @pl.when(group + step < groups)
            def _():
                comp_copy(
                    comp_own, group * within + member,
                    next_comp.at[step * within + member], (group + step, seq),
                ).wait_send()

        return carry

    lax.fori_loop(0, half, finish, 0)

    def sent(distance, carry):
        target = (group, same_parity(distance))
        rows_copy(packed, own_slot, along_rows.at[distance], target).wait_send()
        comp_copy(comp_own, own_comp, along_comp.at[distance], target).wait_send()
        return carry

    lax.fori_loop(1, half, sent, 0)
    keep_rows.wait()
    keep_comp.wait()


def exchange(groups, within, keys, values, key_weight, value_weight):
    length, key_dim = keys.shape
    width = padded(key_dim) + padded(values.shape[1])
    comp_rows = length // key_weight.shape[0]
    dma = pltpu.SemaphoreType.DMA
    vmem = pl.BlockSpec(memory_space=pltpu.VMEM)
    return pl.pallas_call(
        functools.partial(exchange_kernel, groups, within),
        out_shape=(
            jax.ShapeDtypeStruct((2 * within, length, width), keys.dtype),
            jax.ShapeDtypeStruct((groups * within, comp_rows, width), jnp.float32),
        ),
        in_specs=[vmem] * 4,
        out_specs=(pl.BlockSpec(memory_space=pl.ANY), pl.BlockSpec(memory_space=pl.ANY)),
        scratch_shapes=[
            pltpu.VMEM((length, width), keys.dtype),
            pltpu.VMEM((comp_rows, width), jnp.float32),
            dma((2 * within,)),
            dma((groups * within,)),
            dma((within,)),
            dma((within,)),
            dma((2 * within,)),
            dma((groups * within,)),
            dma((within,)),
            dma((groups * within,)),
            dma((2,)),
        ],
        compiler_params=pltpu.CompilerParams(collective_id=0, has_side_effects=True),
        name="exchange",
    )(keys, values, key_weight, value_weight)


def contract(left, right):
    return lax.dot_general(left, right, (((1,), (1,)), ((), ())), preferred_element_type=jnp.float32)


def attend_kernel(
    within, stride, key_dim, heads_step, place, select, queries, gate_logits, table, comp, out,
    rows, gates, sel_keys, sel_values, win_values, comp_parts, comp_high, comp_low,
    sel_bias, win_bias, comp_bias,
):
    group, seq = place[0], place[1]
    length = queries.shape[0]
    tiles, picks = select.shape
    block = length // tiles
    heads = gate_logits.shape[1] // 3
    value_dim = out.shape[1] // heads
    key_room = padded(key_dim)
    comp_count = comp.shape[0]
    group_len = within * length
    win_len = win_bias.shape[1]
    first_place = (group - 1) * group_len
    factor = key_dim ** (-0.5) * 1.4426950408889634
    low = -jnp.inf

    @pl.when(group == 0)
    def _():
        table[:group_len, :] = jnp.zeros((group_len, table.shape[1]), table.dtype)

    comp_here = (lax.broadcasted_iota(jnp.int32, (comp_count, 1), 0) * stride) < (group + 1) * group_len
    source = jnp.where(comp_here, comp[...], 0.0)
    rest = source[:, :key_dim]
    for part in range(3):
        piece = rest.astype(jnp.bfloat16)
        comp_parts[part] = piece
        rest = rest - piece.astype(jnp.float32)
    value_part = source[:, key_room:]
    high = value_part.astype(jnp.bfloat16)
    comp_high[:, :value_dim] = high
    comp_high[:, value_dim:] = jnp.ones((comp_count, LANES), jnp.bfloat16)
    comp_low[...] = (value_part - high.astype(jnp.float32)).astype(jnp.bfloat16)
    sel_values[:, value_dim:] = jnp.ones((picks * block, LANES), jnp.bfloat16)
    win_values[:, value_dim:] = jnp.ones((win_len, LANES), jnp.bfloat16)
    gate_all = jax.nn.sigmoid(gate_logits[...])
    step_rows = heads_step * block

    for tile in range(tiles):
        top = tile * block
        tile_place = (group * within + seq) * length + top
        for head in range(heads):
            rows[head * block : (head + 1) * block, :] = queries[
                top : top + block, head * key_dim : (head + 1) * key_dim
            ]
            for branch in range(3):
                column = branch * heads + head
                gates[branch, head * block : (head + 1) * block, :] = jnp.broadcast_to(
                    gate_all[top : top + block, column : column + 1], (block, LANES)
                )
        for pick in range(picks):
            start = pl.multiple_of(select[tile, pick] * block - first_place, block)
            got = table[pl.ds(start, block), :]
            sel_keys[pick * block : (pick + 1) * block, :] = got[:, :key_room]
            sel_values[pick * block : (pick + 1) * block, :value_dim] = got[:, key_room:]
        lane_all = lax.broadcasted_iota(jnp.int32, (block, picks * block), 1)
        row_place = tile_place + lax.broadcasted_iota(jnp.int32, (block, picks * block), 0)
        shift = jnp.zeros((1, picks * block), jnp.int32)
        lane_one = lax.broadcasted_iota(jnp.int32, (1, picks * block), 1)
        for pick in range(picks):
            inside = (lane_one >= pick * block) & (lane_one < (pick + 1) * block)
            shift = jnp.where(inside, (select[tile, pick] - pick) * block, shift)
        sel_bias[...] = jnp.where(lane_all + shift <= row_place, 0.0, low)
        win_start = pl.multiple_of(group_len + seq * length + top - (win_len - block), block)
        win_place = tile_place - (win_len - block) + lax.broadcasted_iota(jnp.int32, (block, win_len), 1)
        win_row = tile_place + lax.broadcasted_iota(jnp.int32, (block, win_len), 0)
        win_bias[...] = jnp.where(
            (win_place <= win_row) & (win_place > win_row - WINDOW) & (win_place >= 0), 0.0, low
        )
        comp_place = stride * lax.broadcasted_iota(jnp.int32, (block, comp_count), 1)
        comp_row = tile_place + lax.broadcasted_iota(jnp.int32, (block, comp_count), 0)
        comp_bias[...] = jnp.where(comp_place <= comp_row, 0.0, low)
        win_values[:, :value_dim] = table[pl.ds(win_start, win_len), key_room:]

        def weigh(scores, bias):
            scores = scores.reshape(heads_step, block, scores.shape[1]) + bias[...][None]
            top_score = jnp.max(scores, axis=-1, keepdims=True)
            weights = jnp.exp2((scores - top_score) * factor)
            return weights.astype(jnp.bfloat16).reshape(step_rows, scores.shape[2])

        def mix(weights, extended):
            both = jnp.dot(weights, extended, preferred_element_type=jnp.float32)
            return both[:, :value_dim], both[:, value_dim : value_dim + value_dim]

        def some_heads(step, carry):
            here = pl.ds(pl.multiple_of(step * step_rows, step_rows), step_rows)
            query = rows[here, :]
            weights = weigh(contract(query, sel_keys[:, :key_dim]), sel_bias)
            numer, denom = mix(weights, sel_values[...])
            total = gates[1, here, :] * numer / denom
            weights = weigh(contract(query, table[pl.ds(win_start, win_len), :key_dim]), win_bias)
            numer, denom = mix(weights, win_values[...])
            total = total + gates[2, here, :] * numer / denom
            scores = (
                contract(query, comp_parts[0]) + contract(query, comp_parts[1])
            ) + contract(query, comp_parts[2])
            weights = weigh(scores, comp_bias)
            numer, denom = mix(weights, comp_high[...])
            numer = numer + jnp.dot(weights, comp_low[...], preferred_element_type=jnp.float32)
            total = (total + gates[0, here, :] * numer / denom).astype(out.dtype)
            pieces = [total[n * block : (n + 1) * block, :] for n in range(heads_step)]
            columns = pl.ds(pl.multiple_of(step * heads_step * value_dim, LANES), heads_step * value_dim)
            out[top : top + block, columns] = jnp.concatenate(pieces, axis=1)
            return carry

        lax.fori_loop(0, heads // heads_step, some_heads, 0)


def attend(within, stride, key_dim, place, select, queries, gate_logits, table, comp):
    length = queries.shape[0]
    tiles, picks = select.shape
    block = length // tiles
    heads = gate_logits.shape[1] // 3
    value_dim = table.shape[1] - padded(key_dim)
    comp_count = comp.shape[0]
    win_len = WINDOW + block
    sel_len = picks * block
    vmem = pl.BlockSpec(memory_space=pltpu.VMEM)
    smem = pl.BlockSpec(memory_space=pltpu.SMEM)
    bf16, f32 = jnp.bfloat16, jnp.float32
    return pl.pallas_call(
        functools.partial(attend_kernel, within, stride, key_dim, 4),
        out_shape=jax.ShapeDtypeStruct((length, heads * value_dim), queries.dtype),
        in_specs=[smem, smem, vmem, vmem, vmem, vmem],
        out_specs=vmem,
        scratch_shapes=[
            pltpu.VMEM((heads * block, key_dim), bf16),
            pltpu.VMEM((3, heads * block, LANES), f32),
            pltpu.VMEM((sel_len, padded(key_dim)), bf16),
            pltpu.VMEM((sel_len, value_dim + LANES), bf16),
            pltpu.VMEM((win_len, value_dim + LANES), bf16),
            pltpu.VMEM((3, comp_count, key_dim), bf16),
            pltpu.VMEM((comp_count, value_dim + LANES), bf16),
            pltpu.VMEM((comp_count, value_dim), bf16),
            pltpu.VMEM((block, sel_len), f32),
            pltpu.VMEM((block, win_len), f32),
            pltpu.VMEM((block, comp_count), f32),
        ],
        compiler_params=pltpu.CompilerParams(vmem_limit_bytes=56 * 1024 * 1024),
        name="attend",
    )(place, select, queries, gate_logits, table, comp)


def shards(queries, keys, values, comp_key_weight, comp_value_weight, select, gate_logits):
    groups = lax.axis_size("grp")
    within = lax.axis_size("seq")
    place = jnp.stack([lax.axis_index("grp"), lax.axis_index("seq")]).astype(jnp.int32)
    table, comp = exchange(groups, within, keys, values, comp_key_weight, comp_value_weight)
    table = table.reshape(-1, table.shape[2])
    comp = comp.reshape(-1, comp.shape[2])
    return attend(
        within, comp_key_weight.shape[0], keys.shape[1], place, select, queries, gate_logits, table, comp
    )


def solution(mesh):
    return jax.shard_map(
        shards,
        mesh=mesh,
        in_specs=(
            P(("grp", "seq"), None),
            P(("grp", "seq"), None),
            P(("grp", "seq"), None),
            P(),
            P(),
            P(("grp", "seq"), None),
            P(("grp", "seq"), None),
        ),
        out_specs=P(("grp", "seq"), None),
        check_vma=False,
    )
```

profile of v0, /device:TPU:5, one launch (start us, length us, event | category | flops | bytes accessed | tf_op | source)
XLA Modules:
  0.0 40.8 jit_solution(15978147893654103850)
XLA Ops:
  0.0 0.6 %pad_add_fusion.place = s32[2]{0:T(128)} fusion(s32[1]{0:T(128)} %bitcast.1, s32[1]{0:T(128)} %bitcast), kind=kLoop, calls=%fused_computation | loop fusion | flops 2 | bytes 16 | tf_op jit(solution)/shard_map/stack | solution.py:383
  0.6 1.5 %copy.8.keys = bf16[128,192]{1,0:T(8,128)(2,1)} copy(bf16[128,192]{0,1:T(8,128)(2,1)} %param.8) | data formatting | bytes 98304 | tf_op args[1]
  2.1 1.5 %copy.9.gate_logits = f32[128,48]{1,0:T(8,128)} copy(f32[128,48]{0,1:T(8,128)} %param.13) | data formatting | bytes 49152 | tf_op args[6]
  3.5 23.1 %exchange.1 = (bf16[16,128,384]{2,1,0:T(8,128)(2,1)}, f32[32,8,384]{2,1,0:T(8,128)}) custom-call(bf16[128,192]{1,0:T(8,128)(2,1)} %copy.8.keys, bf16[128,128]{1,0:T(8,128)(2,1)} %values.1, f32[16,192]{1,0:T(8,128)} %key_weight.1, f32[16,128]{1,0:T(8,128)} %value_weight.1), custom_call_target="tpu_custom_call" | custom-call | tf_op jit(solution)/shard_map/exchange/pallas_call | solution.py:205
  26.7 14.1 %attend.1 = bf16[128,2048]{1,0:T(8,128)(2,1)} custom-call(s32[2]{0:T(128)} %pad_add_fusion.place, s32[2,16]{1,0:T(2,128)} %select.1, bf16[128,3072]{1,0:T(8,128)(2,1)} %queries.1, f32[128,48]{1,0:T(8,128)} %copy.9.gate_logits, bf16[2048,384]{1,0:T(8,128)(2,1)} %bitcast.4, f32[256,384]{1,0:T(8,128)} %bitcast.5), custom_call_target="tpu_custom_call" | custom-call | tf_op jit(solution)/shard_map/attend/pallas_call | solution.py:357
where the time goes:
time: 41.5 us; the launch traced here: 40.8 us
  Pallas kernels  37.2 us (90%)
  local copies, waits for them, and re-layouts  2.99 us (7%)
  other arithmetic  0.55 us (1%)
    pallas_call x1, Pallas kernels, exchange(): pl.pallas_call(functools.partial(exchange_kernel, groups, within), out_sh...  23.1 us
    pallas_call x1, Pallas kernels, attend(): pl.pallas_call(functools.partial(attend_kernel, within, stride, key_dim,...  14.1 us
    unnamed x2, local copies, waits for them, and re-layouts  2.99 us

commit v1 on v0

--- a/solution.py
+++ b/solution.py
@@ -17,7 +17,7 @@
 
 
 def exchange_kernel(
-    groups, within, keys, values, key_weight, value_weight, table, comp,
+    groups, within, keys_turned, values, key_weight, value_weight, table, comp,
     packed, comp_own, recv_rows, recv_comp, along_rows, along_comp,
     pair_rows, pair_comp, next_rows, next_comp, local_sem,
 ):
@@ -25,11 +25,11 @@
     seq = lax.axis_index("seq")
     half = within // 2
     sibling = seq + 1 - 2 * lax.rem(seq, 2)
-    key_dim = keys.shape[1]
-    value_dim = values.shape[1]
+    length = values.shape[0]
+    key_dim = keys_turned.shape[0]
     key_room = padded(key_dim)
     stride = key_weight.shape[0]
-    comp_rows = keys.shape[0] // stride
+    comp_rows = length // stride
 
     def same_parity(distance):
         return lax.rem(seq + 2 * distance + 2 * within, within)
@@ -48,17 +48,18 @@
         other = lax.rem(group + step, groups)
         pl.semaphore_signal(barrier, inc=1, device_id=(other, seq), device_id_type=MESH)
 
-    packed[:, :key_room] = jnp.zeros((keys.shape[0], key_room), packed.dtype)
-    packed[:, :key_dim] = keys[...]
+    keys = keys_turned[...].T
+    packed[:, :key_room] = jnp.zeros((length, key_room), packed.dtype)
+    packed[:, :key_dim] = keys
     packed[:, key_room:] = values[...]
     comp_own[...] = jnp.zeros_like(comp_own)
 
     def summed(source, weight):
-        wide = source[...].astype(jnp.float32).reshape(comp_rows, stride, source.shape[1])
+        wide = source.astype(jnp.float32).reshape(comp_rows, stride, source.shape[1])
         return jnp.sum(wide * weight[...][None], axis=1)
 
     comp_own[:, :key_dim] = summed(keys, key_weight)
-    comp_own[:, key_room:] = summed(values, value_weight)
+    comp_own[:, key_room:] = summed(values[...], value_weight)
     pl.semaphore_wait(barrier, half - 1 + 1 + groups - 1)
 
     def rows_copy(source, slot, send_sem, target):
@@ -225,7 +226,7 @@
         ],
         compiler_params=pltpu.CompilerParams(collective_id=0, has_side_effects=True),
         name="exchange",
-    )(keys, values, key_weight, value_weight)
+    )(keys.T, values, key_weight, value_weight)
 
 
 def contract(left, right):
@@ -233,15 +234,15 @@
 
 
 def attend_kernel(
-    within, stride, key_dim, heads_step, place, select, queries, gate_logits, table, comp, out,
+    within, stride, key_dim, heads_step, select, queries, gate_logits, table, comp, out,
     rows, gates, sel_keys, sel_values, win_values, comp_parts, comp_high, comp_low,
     sel_bias, win_bias, comp_bias,
 ):
-    group, seq = place[0], place[1]
+    group, seq = lax.axis_index("grp"), lax.axis_index("seq")
     length = queries.shape[0]
     tiles, picks = select.shape
     block = length // tiles
-    heads = gate_logits.shape[1] // 3
+    heads = gate_logits.shape[0] // 3
     value_dim = out.shape[1] // heads
     key_room = padded(key_dim)
     comp_count = comp.shape[0]
@@ -269,7 +270,7 @@
     comp_low[...] = (value_part - high.astype(jnp.float32)).astype(jnp.bfloat16)
     sel_values[:, value_dim:] = jnp.ones((picks * block, LANES), jnp.bfloat16)
     win_values[:, value_dim:] = jnp.ones((win_len, LANES), jnp.bfloat16)
-    gate_all = jax.nn.sigmoid(gate_logits[...])
+    gate_all = jax.nn.sigmoid(gate_logits[...]).T
     step_rows = heads_step * block
 
     for tile in range(tiles):
@@ -342,7 +343,7 @@
         lax.fori_loop(0, heads // heads_step, some_heads, 0)
 
 
-def attend(within, stride, key_dim, place, select, queries, gate_logits, table, comp):
+def attend(within, stride, key_dim, select, queries, gate_logits, table, comp):
     length = queries.shape[0]
     tiles, picks = select.shape
     block = length // tiles
@@ -357,7 +358,7 @@
     return pl.pallas_call(
         functools.partial(attend_kernel, within, stride, key_dim, 4),
         out_shape=jax.ShapeDtypeStruct((length, heads * value_dim), queries.dtype),
-        in_specs=[smem, smem, vmem, vmem, vmem, vmem],
+        in_specs=[smem, vmem, vmem, vmem, vmem],
         out_specs=vmem,
         scratch_shapes=[
             pltpu.VMEM((heads * block, key_dim), bf16),
@@ -374,18 +375,17 @@
         ],
         compiler_params=pltpu.CompilerParams(vmem_limit_bytes=56 * 1024 * 1024),
         name="attend",
-    )(place, select, queries, gate_logits, table, comp)
+    )(select, queries, gate_logits.T, table, comp)
 
 
 def shards(queries, keys, values, comp_key_weight, comp_value_weight, select, gate_logits):
     groups = lax.axis_size("grp")
     within = lax.axis_size("seq")
-    place = jnp.stack([lax.axis_index("grp"), lax.axis_index("seq")]).astype(jnp.int32)
     table, comp = exchange(groups, within, keys, values, comp_key_weight, comp_value_weight)
     table = table.reshape(-1, table.shape[2])
     comp = comp.reshape(-1, comp.shape[2])
     return attend(
-        within, comp_key_weight.shape[0], keys.shape[1], place, select, queries, gate_logits, table, comp
+        within, comp_key_weight.shape[0], keys.shape[1], select, queries, gate_logits, table, comp
     )
 
 

time: 41.5 us -> 37.9 us (0.913)
  local copies, waits for them, and re-layouts: 2.99 us -> 0 us
  other arithmetic: 0.55 us -> 0 us
    unnamed x2 -> x0, local copies, waits for them, and re-layouts: 2.99 us -> none
    another operation x1 -> x0, other arithmetic: 0.55 us -> none  [shards(): jnp.stack([lax.axis_index('grp'), lax.axis_index('seq')]).astype(jnp.int32)]
where the time goes in v1:
time: 37.9 us; the launch traced here: 37.3 us
  Pallas kernels  37.3 us (98%)
    pallas_call x1, Pallas kernels, exchange(): pl.pallas_call(functools.partial(exchange_kernel, groups, within), out_sh...  23.1 us
    pallas_call x1, Pallas kernels, attend(): pl.pallas_call(functools.partial(attend_kernel, within, stride, key_dim,...  14.3 us

profile of v1, /device:TPU:5, one launch (start us, length us, event | category | flops | bytes accessed | tf_op | source)
XLA Modules:
  0.0 37.3 jit_solution(15285605341523657660)
XLA Ops:
  0.0 23.1 %exchange.1 = (bf16[16,128,384]{2,1,0:T(8,128)(2,1)}, f32[32,8,384]{2,1,0:T(8,128)}) custom-call(bf16[192,128]{1,0:T(8,128)(2,1)} %bitcast.6, bf16[128,128]{1,0:T(8,128)(2,1)} %values.1, f32[16,192]{1,0:T(8,128)} %key_weight.1, f32[16,128]{1,0:T(8,128)} %value_weight.1), custom_call_target="tpu_custom_call" | custom-call | tf_op jit(solution)/shard_map/exchange/pallas_call | solution.py:206
  23.1 14.3 %attend.1 = bf16[128,2048]{1,0:T(8,128)(2,1)} custom-call(s32[2,16]{1,0:T(2,128)} %select.1, bf16[128,3072]{1,0:T(8,128)(2,1)} %queries.1, f32[48,128]{1,0:T(8,128)} %bitcast.7, bf16[2048,384]{1,0:T(8,128)(2,1)} %bitcast.4, f32[256,384]{1,0:T(8,128)} %bitcast.5), custom_call_target="tpu_custom_call" | custom-call | tf_op jit(solution)/shard_map/attend/pallas_call | solution.py:358

commit v2 on v1

v2 whole, which is shorter than its diff:
```python
import functools

import jax
import jax.numpy as jnp
from jax import lax
from jax.experimental import pallas as pl
from jax.experimental.pallas import tpu as pltpu
from jax.sharding import PartitionSpec as P

WINDOW = 512
LANES = 128
MESH = pl.DeviceIdType.MESH


def padded(width):
    return -(-width // LANES) * LANES


def fused_kernel(
    groups, within, heads_step, queries, keys_turned, values, key_weight, value_weight, select,
    gate_logits, out, table, comp, recv_rows, recv_comp, along_rows, along_comp,
    pair_rows, pair_comp, next_rows, next_comp,
    rows, gates, total, sel_keys, sel_values, win_values, comp_parts, comp_high, comp_low,
    sel_bias, win_bias, comp_bias,
):
    group = lax.axis_index("grp")
    seq = lax.axis_index("seq")
    half = within // 2
    sibling = seq + 1 - 2 * lax.rem(seq, 2)
    length = values.shape[0]
    key_dim = keys_turned.shape[0]
    key_room = padded(key_dim)
    stride = key_weight.shape[0]
    comp_rows = length // stride
    tiles, picks = select.shape
    block = length // tiles
    heads = gate_logits.shape[0] // 3
    value_dim = values.shape[1]
    comp_count = comp.shape[0]
    win_len = win_bias.shape[2]
    first_block = (group - 1) * within * tiles
    win_blocks = win_len // block
    factor = key_dim ** (-0.5) * 1.4426950408889634
    low = -jnp.inf
    step_rows = heads_step * block
    steps = heads // heads_step

    def table_at(slot):
        return table.at[pl.ds(slot * tiles, tiles)]

    def comp_at(slot):
        return comp.at[pl.ds(pl.multiple_of(slot * comp_rows, comp_rows), comp_rows)]

    def same_parity(distance):
        return lax.rem(seq + 2 * distance + 2 * within, within)

    barrier = pltpu.get_barrier_semaphore()

    def greet(distance, carry):
        pl.semaphore_signal(
            barrier, inc=1, device_id=(group, same_parity(distance)), device_id_type=MESH
        )
        return carry

    lax.fori_loop(1, half, greet, 0)
    pl.semaphore_signal(barrier, inc=1, device_id=(group, sibling), device_id_type=MESH)
    for step in range(1, groups):
        other = lax.rem(group + step, groups)
        pl.semaphore_signal(barrier, inc=1, device_id=(other, seq), device_id_type=MESH)

    own_slot = within + seq
    own_comp = group * within + seq
    own_rows = pl.ds(own_slot * tiles, tiles)
    own_comp_rows = pl.ds(pl.multiple_of(own_comp * comp_rows, comp_rows), comp_rows)
    keys = keys_turned[...].T
    table[own_rows, :, :key_room] = jnp.zeros((tiles, block, key_room), table.dtype)
    table[own_rows, :, :key_dim] = keys.reshape(tiles, block, key_dim)
    table[own_rows, :, key_room:] = values[...].reshape(tiles, block, value_dim)
    comp[own_comp_rows, :] = jnp.zeros((comp_rows, comp.shape[1]), jnp.float32)

    def summed(source, weight):
        wide = source.astype(jnp.float32).reshape(comp_rows, stride, source.shape[1])
        return jnp.sum(wide * weight[...][None], axis=1)

    comp[own_comp_rows, :key_dim] = summed(keys, key_weight)
    comp[own_comp_rows, key_room:] = summed(values[...], value_weight)
    @pl.when(group == 0)
    def _():
        table[: within * tiles] = jnp.zeros((within * tiles, block, table.shape[2]), table.dtype)

    group_comp = within * comp_rows
    for later in range(1, groups):
        @pl.when(group < later)
        def _():
            comp[later * group_comp : (later + 1) * group_comp, :] = jnp.zeros(
                (group_comp, comp.shape[1]), jnp.float32
            )

    pl.semaphore_wait(barrier, half - 1 + 1 + groups - 1)

    def rows_copy(source, slot, send_sem, target):
        return pltpu.make_async_remote_copy(
            src_ref=source, dst_ref=table_at(slot), send_sem=send_sem,
            recv_sem=recv_rows.at[slot], device_id=target, device_id_type=MESH,
        )

    def comp_copy(source, slot, send_sem, target):
        return pltpu.make_async_remote_copy(
            src_ref=source, dst_ref=comp_at(slot), send_sem=send_sem,
            recv_sem=recv_comp.at[slot], device_id=target, device_id_type=MESH,
        )

    def rows_next(source, member):
        @pl.when(group < groups - 1)
        def _():
            rows_copy(source, member, next_rows.at[member], (group + 1, seq)).start()

    def comp_next(source, member):
        for step in range(1, groups):
            @pl.when(group + step < groups)
            def _():
                comp_copy(
                    source, group * within + member,
                    next_comp.at[step * within + member], (group + step, seq),
                ).start()

    packed = table_at(own_slot)
    comp_own = comp_at(own_comp)

    def spread_comp(distance, carry):
        target = (group, same_parity(distance))
        comp_copy(comp_own, own_comp, along_comp.at[distance], target).start()
        return carry

    def spread_rows(distance, carry):
        target = (group, same_parity(distance))
        rows_copy(packed, own_slot, along_rows.at[distance], target).start()
        return carry

    lax.fori_loop(1, half, spread_comp, 0)
    comp_next(comp_own, seq)
    comp_copy(comp_own, own_comp, pair_comp.at[own_comp], (group, sibling)).start()
    lax.fori_loop(1, half, spread_rows, 0)
    rows_next(packed, seq)
    rows_copy(packed, own_slot, pair_rows.at[own_slot], (group, sibling)).start()

    def arrive_rows(slot):
        rows_copy(packed, slot, pair_rows.at[slot], (group, sibling)).wait_recv()

    def arrive_comp(slot):
        comp_copy(comp_own, slot, pair_comp.at[slot], (group, sibling)).wait_recv()

    def stage(tile):
        top = tile * block
        tile_place = (group * within + seq) * length + top
        for head in range(heads):
            rows[tile, head * block : (head + 1) * block, :] = queries[
                top : top + block, head * key_dim : (head + 1) * key_dim
            ]
            for branch in range(3):
                column = branch * heads + head
                gates[tile, branch, head * block : (head + 1) * block, :] = jnp.broadcast_to(
                    gate_all[top : top + block, column : column + 1], (block, LANES)
                )
        lane_all = lax.broadcasted_iota(jnp.int32, (block, picks * block), 1)
        row_place = tile_place + lax.broadcasted_iota(jnp.int32, (block, picks * block), 0)
        shift = jnp.zeros((1, picks * block), jnp.int32)
        lane_one = lax.broadcasted_iota(jnp.int32, (1, picks * block), 1)
        for pick in range(picks):
            inside = (lane_one >= pick * block) & (lane_one < (pick + 1) * block)
            shift = jnp.where(inside, (select[tile, pick] - pick) * block, shift)
        sel_bias[tile] = jnp.where(lane_all + shift <= row_place, 0.0, low)
        win_place = tile_place - (win_len - block) + lax.broadcasted_iota(jnp.int32, (block, win_len), 1)
        win_row = tile_place + lax.broadcasted_iota(jnp.int32, (block, win_len), 0)
        win_bias[tile] = jnp.where(
            (win_place <= win_row) & (win_place > win_row - WINDOW) & (win_place >= 0), 0.0, low
        )
        comp_place = stride * lax.broadcasted_iota(jnp.int32, (block, comp_count), 1)
        comp_row = tile_place + lax.broadcasted_iota(jnp.int32, (block, comp_count), 0)
        comp_bias[tile] = jnp.where(comp_place <= comp_row, 0.0, low)
        sel_values[tile, :, value_dim:] = jnp.ones((picks * block, LANES), jnp.bfloat16)

    def weigh(scores, bias):
        scores = scores.reshape(heads_step, block, scores.shape[1]) + bias[None]
        top_score = jnp.max(scores, axis=-1, keepdims=True)
        weights = jnp.exp2((scores - top_score) * factor)
        return weights.astype(jnp.bfloat16).reshape(step_rows, scores.shape[2])

    def mix(weights, extended):
        both = jnp.dot(weights, extended, preferred_element_type=jnp.float32)
        return both[:, :value_dim], both[:, value_dim : value_dim + value_dim]

    def step_at(step):
        return pl.ds(pl.multiple_of(step * step_rows, step_rows), step_rows)

    def comp_unit(unit, carry):
        tile, here = unit // steps, step_at(unit % steps)
        query = rows[tile, here, :]
        scores = (
            contract(query, comp_parts[0]) + contract(query, comp_parts[1])
        ) + contract(query, comp_parts[2])
        weights = weigh(scores, comp_bias[tile])
        numer, denom = mix(weights, comp_high[...])
        numer = numer + jnp.dot(weights, comp_low[...], preferred_element_type=jnp.float32)
        total[tile, here, :] = gates[tile, 0, here, :] * numer / denom
        return carry

    def relay_comp(distance, carry):
        member = same_parity(-distance)
        slot = group * within + member
        arrive_comp(slot)
        comp_next(comp_at(slot), member)
        comp_copy(comp_at(slot), slot, pair_comp.at[slot], (group, sibling)).start()
        return carry

    def relay_prior_comp(distance, carry):
        member = same_parity(-distance)
        for step in range(1, groups):
            @pl.when(group >= step)
            def _():
                slot = (group - step) * within + member
                arrive_comp(slot)
                comp_copy(comp_at(slot), slot, pair_comp.at[slot], (group, sibling)).start()

        return carry

    def finish_comp(distance, carry):
        other = same_parity(distance) + sibling - seq
        arrive_comp(group * within + other)
        for step in range(1, groups):
            @pl.when(group >= step)
            def _():
                arrive_comp((group - step) * within + other)

        return carry

    def relay_rows(distance):
        member = same_parity(-distance)
        slot = within + member
        arrive_rows(slot)
        rows_next(table_at(slot), member)
        rows_copy(table_at(slot), slot, pair_rows.at[slot], (group, sibling)).start()

    def relay_prior_rows(distance, carry):
        member = same_parity(-distance)

        @pl.when(group > 0)
        def _():
            arrive_rows(member)
            rows_copy(table_at(member), member, pair_rows.at[member], (group, sibling)).start()

        return carry

    def finish_rows(distance, carry):
        other = same_parity(distance) + sibling - seq
        arrive_rows(within + other)

        @pl.when(group > 0)
        def _():
            arrive_rows(other)

        return carry

    gate_all = jax.nn.sigmoid(gate_logits[...]).T
    stage(0)
    lax.fori_loop(1, half, relay_comp, 0)
    for tile in range(1, tiles):
        stage(tile)
    win_values[:, value_dim:] = jnp.ones((win_len, LANES), jnp.bfloat16)
    comp_high[:, value_dim:] = jnp.ones((comp_count, LANES), jnp.bfloat16)
    lax.fori_loop(0, half, relay_prior_comp, 0)
    if half > 1:
        relay_rows(1)
    lax.fori_loop(0, half, finish_comp, 0)
    rest = comp[:, :key_dim]
    for part in range(3):
        piece = rest.astype(jnp.bfloat16)
        comp_parts[part] = piece
        rest = rest - piece.astype(jnp.float32)
    value_part = comp[:, key_room:]
    high = value_part.astype(jnp.bfloat16)
    comp_high[:, :value_dim] = high
    comp_low[...] = (value_part - high.astype(jnp.float32)).astype(jnp.bfloat16)
    units = tiles * steps
    spans = max(half - 1, 1)

    def relay_and_weigh(distance, carry):
        relay_rows(distance)
        lax.fori_loop(units * (distance - 2) // spans, units * (distance - 1) // spans, comp_unit, 0)
        return carry

    lax.fori_loop(2, half, relay_and_weigh, 0)
    lax.fori_loop(units * max(half - 2, 0) // spans, units, comp_unit, 0)
    lax.fori_loop(0, half, relay_prior_rows, 0)
    lax.fori_loop(0, half, finish_rows, 0)

    for tile in range(tiles):
        top = tile * block
        for pick in range(picks):
            got = table[jnp.clip(select[tile, pick] - first_block, 0, 2 * within * tiles - 1)]
            sel_keys[pick * block : (pick + 1) * block, :] = got[:, :key_room]
            sel_values[tile, pick * block : (pick + 1) * block, :value_dim] = got[:, key_room:]
        win_here = pl.ds(within * tiles + seq * tiles + tile - (win_blocks - 1), win_blocks)
        win_values[:, :value_dim] = table[win_here, :, key_room:].reshape(win_len, value_dim)

        def some_heads(step, carry):
            here = step_at(step)
            query = rows[tile, here, :]
            weights = weigh(contract(query, sel_keys[:, :key_dim]), sel_bias[tile])
            numer, denom = mix(weights, sel_values[tile])
            result = total[tile, here, :] + gates[tile, 1, here, :] * numer / denom
            weights = weigh(contract(query, table[win_here, :, :key_dim].reshape(win_len, key_dim)), win_bias[tile])
            numer, denom = mix(weights, win_values[...])
            result = (result + gates[tile, 2, here, :] * numer / denom).astype(out.dtype)
            pieces = [result[n * block : (n + 1) * block, :] for n in range(heads_step)]
            columns = pl.ds(pl.multiple_of(step * heads_step * value_dim, LANES), heads_step * value_dim)
            out[top : top + block, columns] = jnp.concatenate(pieces, axis=1)
            return carry

        lax.fori_loop(0, steps, some_heads, 0)

    def sent_here(distance, carry):
        member = same_parity(distance)
        rows_copy(packed, within + member, pair_rows.at[within + member], (group, sibling)).wait_send()
        comp_copy(
            comp_own, group * within + member, pair_comp.at[group * within + member], (group, sibling)
        ).wait_send()

        @pl.when(group > 0)
        def _():
            rows_copy(packed, member, pair_rows.at[member], (group, sibling)).wait_send()

        @pl.when(group < groups - 1)
        def _():
            rows_copy(packed, member, next_rows.at[member], (group + 1, seq)).wait_send()

        for step in range(1, groups):
            @pl.when(group >= step)
            def _():
                slot = (group - step) * within + member
                comp_copy(comp_own, slot, pair_comp.at[slot], (group, sibling)).wait_send()

            @pl.when(group + step < groups)
            def _():
                comp_copy(
                    comp_own, group * within + member,
                    next_comp.at[step * within + member], (group + step, seq),
                ).wait_send()

        return carry

    lax.fori_loop(0, half, sent_here, 0)

    def sent_along(distance, carry):
        target = (group, same_parity(distance))
        rows_copy(packed, own_slot, along_rows.at[distance], target).wait_send()
        comp_copy(comp_own, own_comp, along_comp.at[distance], target).wait_send()
        return carry

    lax.fori_loop(1, half, sent_along, 0)


def contract(left, right):
    return lax.dot_general(left, right, (((1,), (1,)), ((), ())), preferred_element_type=jnp.float32)


def shards(queries, keys, values, comp_key_weight, comp_value_weight, select, gate_logits):
    groups = lax.axis_size("grp")
    within = lax.axis_size("seq")
    length, key_dim = keys.shape
    value_dim = values.shape[1]
    tiles, picks = select.shape
    block = length // tiles
    heads = gate_logits.shape[1] // 3
    width = padded(key_dim) + padded(value_dim)
    comp_rows = length // comp_key_weight.shape[0]
    comp_count = groups * within * comp_rows
    win_len = WINDOW + block
    sel_len = picks * block
    dma = pltpu.SemaphoreType.DMA
    vmem = pl.BlockSpec(memory_space=pltpu.VMEM)
    smem = pl.BlockSpec(memory_space=pltpu.SMEM)
    bf16, f32 = jnp.bfloat16, jnp.float32
    return pl.pallas_call(
        functools.partial(fused_kernel, groups, within, 4),
        out_shape=jax.ShapeDtypeStruct((length, heads * value_dim), queries.dtype),
        in_specs=[vmem, vmem, vmem, vmem, vmem, smem, vmem],
        out_specs=vmem,
        scratch_shapes=[
            pltpu.VMEM((2 * within * tiles, block, width), bf16),
            pltpu.VMEM((comp_count, width), f32),
            dma((2 * within,)),
            dma((groups * within,)),
            dma((within,)),
            dma((within,)),
            dma((2 * within,)),
            dma((groups * within,)),
            dma((within,)),
            dma((groups * within,)),
            pltpu.VMEM((tiles, heads * block, key_dim), bf16),
            pltpu.VMEM((tiles, 3, heads * block, LANES), f32),
            pltpu.VMEM((tiles, heads * block, value_dim), f32),
            pltpu.VMEM((sel_len, padded(key_dim)), bf16),
            pltpu.VMEM((tiles, sel_len, value_dim + LANES), bf16),
            pltpu.VMEM((win_len, value_dim + LANES), bf16),
            pltpu.VMEM((3, comp_count, key_dim), bf16),
            pltpu.VMEM((comp_count, value_dim + LANES), bf16),
            pltpu.VMEM((comp_count, value_dim), bf16),
            pltpu.VMEM((tiles, block, sel_len), f32),
            pltpu.VMEM((tiles, block, win_len), f32),
            pltpu.VMEM((tiles, block, comp_count), f32),
        ],
        compiler_params=pltpu.CompilerParams(
            collective_id=0, has_side_effects=True, vmem_limit_bytes=56 * 1024 * 1024
        ),
        name="attend",
    )(queries, keys.T, values, comp_key_weight, comp_value_weight, select, gate_logits.T)


def solution(mesh):
    return jax.shard_map(
        shards,
        mesh=mesh,
        in_specs=(
            P(("grp", "seq"), None),
            P(("grp", "seq"), None),
            P(("grp", "seq"), None),
            P(),
            P(),
            P(("grp", "seq"), None),
            P(("grp", "seq"), None),
        ),
        out_specs=P(("grp", "seq"), None),
        check_vma=False,
    )
```

time: 37.9 us -> 35.9 us (0.947); the launches traced: 37.3 us -> 35.7 us
  Pallas kernels: 37.3 us -> 33.9 us
  local copies, waits for them, and re-layouts: 0 us -> 1.88 us
    pallas_call x2 -> x1, Pallas kernels: 37.3 us -> 33.9 us  [shards(): pl.pallas_call(functools.partial(fused_kernel, groups, within, 4), out_sh...]
    unnamed x0 -> x1, local copies, waits for them, and re-layouts: none -> 1.88 us
where the time goes in v2:
time: 35.9 us; the launch traced here: 35.7 us
  Pallas kernels  33.9 us (94%)
  local copies, waits for them, and re-layouts  1.88 us (5%)
    pallas_call x1, Pallas kernels, shards(): pl.pallas_call(functools.partial(fused_kernel, groups, within, 4), out_sh...  33.9 us
    unnamed x1, local copies, waits for them, and re-layouts  1.88 us

profile of v2, /device:TPU:5, one launch (start us, length us, event | category | flops | bytes accessed | tf_op | source)
XLA Modules:
  0.0 35.7 jit_solution(5353240727043427543)
XLA Ops:
  0.0 33.9 %attend.1 = bf16[128,2048]{1,0:T(8,128)(2,1)} custom-call(bf16[128,3072]{1,0:T(8,128)(2,1)} %queries.1, bf16[192,128]{1,0:T(8,128)(2,1)} %bitcast.2, bf16[128,128]{1,0:T(8,128)(2,1)} %values.1, f32[16,192]{1,0:T(8,128)} %key_weight.1, f32[16,128]{1,0:T(8,128)} %value_weight.1, s32[2,16]{1,0:T(2,128)} %select.1, f32[48,128]{1,0:T(8,128)} %bitcast.3), custom_call_target="tpu_custom_call" | custom-call | tf_op jit(solution)/shard_map/attend/pallas_call | solution.py:384
  33.9 1.9 %copy.9 = bf16[128,2048]{1,0:T(8,128)(2,1)} copy(bf16[128,2048]{1,0:T(8,128)(2,1)} %attend.1) | data formatting | bytes 1048576

commit v3 on v2

--- a/solution.py
+++ b/solution.py
@@ -268,9 +268,13 @@
         stage(tile)
     win_values[:, value_dim:] = jnp.ones((win_len, LANES), jnp.bfloat16)
     comp_high[:, value_dim:] = jnp.ones((comp_count, LANES), jnp.bfloat16)
+
+    def relay_near(distance, carry):
+        relay_rows(distance)
+        return carry
+
+    lax.fori_loop(1, half, relay_near, 0)
     lax.fori_loop(0, half, relay_prior_comp, 0)
-    if half > 1:
-        relay_rows(1)
     lax.fori_loop(0, half, finish_comp, 0)
     rest = comp[:, :key_dim]
     for part in range(3):
@@ -282,16 +286,12 @@
     comp_high[:, :value_dim] = high
     comp_low[...] = (value_part - high.astype(jnp.float32)).astype(jnp.bfloat16)
     units = tiles * steps
-    spans = max(half - 1, 1)
 
     def relay_and_weigh(distance, carry):
-        relay_rows(distance)
-        lax.fori_loop(units * (distance - 2) // spans, units * (distance - 1) // spans, comp_unit, 0)
-        return carry
-
-    lax.fori_loop(2, half, relay_and_weigh, 0)
-    lax.fori_loop(units * max(half - 2, 0) // spans, units, comp_unit, 0)
-    lax.fori_loop(0, half, relay_prior_rows, 0)
+        lax.fori_loop(units * distance // half, units * (distance + 1) // half, comp_unit, 0)
+        return relay_prior_rows(distance, carry)
+
+    lax.fori_loop(0, half, relay_and_weigh, 0)
     lax.fori_loop(0, half, finish_rows, 0)
 
     for tile in range(tiles):
@@ -382,7 +382,7 @@
     smem = pl.BlockSpec(memory_space=pltpu.SMEM)
     bf16, f32 = jnp.bfloat16, jnp.float32
     return pl.pallas_call(
-        functools.partial(fused_kernel, groups, within, 4),
+        functools.partial(fused_kernel, groups, within, 8),
         out_shape=jax.ShapeDtypeStruct((length, heads * value_dim), queries.dtype),
         in_specs=[vmem, vmem, vmem, vmem, vmem, smem, vmem],
         out_specs=vmem,

time: 35.9 us -> 32.9 us (0.916); the launches traced: 35.7 us -> 32.2 us
  Pallas kernels: 33.9 us -> 30.3 us
    pallas_call x1, Pallas kernels: 33.9 us -> 30.3 us  [shards(): pl.pallas_call(functools.partial(fused_kernel, groups, within, 8), out_sh...]
where the time goes in v3:
time: 32.9 us; the launch traced here: 32.2 us
  Pallas kernels  30.3 us (92%)
  local copies, waits for them, and re-layouts  1.88 us (6%)
    pallas_call x1, Pallas kernels, shards(): pl.pallas_call(functools.partial(fused_kernel, groups, within, 8), out_sh...  30.3 us
    unnamed x1, local copies, waits for them, and re-layouts  1.88 us

profile of v3, /device:TPU:5, one launch (start us, length us, event | category | flops | bytes accessed | tf_op | source)
XLA Modules:
  0.0 32.2 jit_solution(4510722249569142372)
XLA Ops:
  0.0 30.3 %attend.1 = bf16[128,2048]{1,0:T(8,128)(2,1)} custom-call(bf16[128,3072]{1,0:T(8,128)(2,1)} %queries.1, bf16[192,128]{1,0:T(8,128)(2,1)} %bitcast.2, bf16[128,128]{1,0:T(8,128)(2,1)} %values.1, f32[16,192]{1,0:T(8,128)} %key_weight.1, f32[16,128]{1,0:T(8,128)} %value_weight.1, s32[2,16]{1,0:T(2,128)} %select.1, f32[48,128]{1,0:T(8,128)} %bitcast.3), custom_call_target="tpu_custom_call" | custom-call | tf_op jit(solution)/shard_map/attend/pallas_call | solution.py:384
  30.3 1.9 %copy.9 = bf16[128,2048]{1,0:T(8,128)(2,1)} copy(bf16[128,2048]{1,0:T(8,128)(2,1)} %attend.1) | data formatting | bytes 1048576

commit v4 on v3

--- a/solution.py
+++ b/solution.py
@@ -288,8 +288,8 @@
     units = tiles * steps
 
     def relay_and_weigh(distance, carry):
-        lax.fori_loop(units * distance // half, units * (distance + 1) // half, comp_unit, 0)
-        return relay_prior_rows(distance, carry)
+        relay_prior_rows(distance, carry)
+        return lax.fori_loop(units * distance // half, units * (distance + 1) // half, comp_unit, carry)
 
     lax.fori_loop(0, half, relay_and_weigh, 0)
     lax.fori_loop(0, half, finish_rows, 0)
@@ -382,7 +382,7 @@
     smem = pl.BlockSpec(memory_space=pltpu.SMEM)
     bf16, f32 = jnp.bfloat16, jnp.float32
     return pl.pallas_call(
-        functools.partial(fused_kernel, groups, within, 8),
+        functools.partial(fused_kernel, groups, within, 16),
         out_shape=jax.ShapeDtypeStruct((length, heads * value_dim), queries.dtype),
         in_specs=[vmem, vmem, vmem, vmem, vmem, smem, vmem],
         out_specs=vmem,

time: 32.9 us -> 30.7 us (0.933); the launches traced: 32.2 us -> 30.5 us
  Pallas kernels: 30.3 us -> 28.6 us
    pallas_call x1, Pallas kernels: 30.3 us -> 28.6 us  [shards(): pl.pallas_call(functools.partial(fused_kernel, groups, within, 16), out_s...]
where the time goes in v4:
time: 30.7 us; the launch traced here: 30.5 us
  Pallas kernels  28.6 us (93%)
  local copies, waits for them, and re-layouts  1.88 us (6%)
    pallas_call x1, Pallas kernels, shards(): pl.pallas_call(functools.partial(fused_kernel, groups, within, 16), out_s...  28.6 us
    unnamed x1, local copies, waits for them, and re-layouts  1.88 us

profile of v4, /device:TPU:5, one launch (start us, length us, event | category | flops | bytes accessed | tf_op | source)
XLA Modules:
  0.0 30.5 jit_solution(17463570293072181349)
XLA Ops:
  0.0 28.6 %attend.1 = bf16[128,2048]{1,0:T(8,128)(2,1)} custom-call(bf16[128,3072]{1,0:T(8,128)(2,1)} %queries.1, bf16[192,128]{1,0:T(8,128)(2,1)} %bitcast.2, bf16[128,128]{1,0:T(8,128)(2,1)} %values.1, f32[16,192]{1,0:T(8,128)} %key_weight.1, f32[16,128]{1,0:T(8,128)} %value_weight.1, s32[2,16]{1,0:T(2,128)} %select.1, f32[48,128]{1,0:T(8,128)} %bitcast.3), custom_call_target="tpu_custom_call" | custom-call | tf_op jit(solution)/shard_map/attend/pallas_call | solution.py:384
  28.6 1.9 %copy.9 = bf16[128,2048]{1,0:T(8,128)(2,1)} copy(bf16[128,2048]{1,0:T(8,128)(2,1)} %attend.1) | data formatting | bytes 1048576
